TPU v7x, 128 devices: a whole 4x4x4 slice. The times are simulated.
128 devices in a mesh: tile: 32 (over z, x, core), group: 4 (over y).
Axes of the slice: x: 4, y: 4, z: 4, core: 2. Of those that a mesh axis runs over, the one named last changes fastest.
Arguments:
- latent: bfloat16 [16, 64, 160, 384], P('group', 'tile'), may hold values from -6 to 6
- tile_rows: int32 [32], replicated, may hold values from 1 to 2, 56 in all
- gain_first: float32 [384], replicated, may hold values from 0.1 to 1.9
- kernel_first: bfloat16 [3, 3, 3, 384, 384], replicated, may hold values from -0.0625 to 0.0625
- gain_second: float32 [384], replicated, may hold values from 0.1 to 1.9
- kernel_second: bfloat16 [3, 3, 3, 384, 384], replicated, may hold values from -0.0625 to 0.0625
Outputs:
- decoded: bfloat16 [16, 64, 160, 384], P('group', 'tile')
Inputs may be any that keep to these rules, and one draw needn't show every extreme that they name: tile_rows sum to 56.
All inputs are finite; a program needn't handle non-finite values.
Results may differ from a plain program's by a relative error of at most 0.004.
Values may be sent and summed in bfloat16 or wider, within the bound.
A program may use at most 256 MiB of HBM per device.

v0:
```python
import functools

import jax
import jax.numpy as jnp
from jax import lax
from jax.experimental import pallas as pl
from jax.experimental.pallas import tpu as pltpu
from jax.sharding import PartitionSpec as P

MESH = pl.DeviceIdType.MESH
cat = jnp.concatenate
F32 = jnp.float32
BF16 = jnp.bfloat16


def activate(values, gain, live):
    scale = lax.rsqrt(jnp.mean(values * values, axis=-1, keepdims=True) + 1e-06)
    u = values * scale * gain
    return (u / (1.0 + jnp.exp(-u))) * live


def shift_sum(before, here, after):
    columns = here.shape[0]
    place = lax.broadcasted_iota(jnp.int32, here.shape, 0)
    left = jnp.where(place == 0, 0.0, pltpu.roll(before, 1, 0))
    right = jnp.where(place == columns - 1, 0.0, pltpu.roll(after, columns - 1, 0))
    return left + here + right


def own_rows(x, w, frame, tap):
    _, _, columns, channels = x.shape
    lhs = cat([x[frame + tap : frame + tap + 2, r].reshape(2 * columns, channels) for r in (1, 2)], axis=1)
    rhs = cat([cat([w[tap, r - out, l] for out in (0, 1) for l in range(3)], axis=1) for r in (1, 2)], axis=0)
    return jnp.dot(lhs, rhs, preferred_element_type=F32)


def halo_row(x, w, frame, out):
    _, _, columns, channels = x.shape
    lhs = cat([x[frame + i : frame + i + 2, 3 * out].reshape(2 * columns, channels) for i in range(3)], axis=1)
    rhs = cat([cat([w[i, 2 * out, l] for l in range(3)], axis=1) for i in range(3)], axis=0)
    return jnp.dot(lhs, rhs, preferred_element_type=F32)


def kernel(
    tiles, groups,
    latent, tile_rows, gain_first, kernel_first, gain_second, kernel_second,
    decoded,
    xa, xb, wa, wb, lat, acc, outv,
    lat_sem, w_sem, out_sem, send_y, recv_y, send_r, recv_r,
):
    frames, rows, columns, channels = lat.shape
    tile = lax.axis_index("tile")
    group = lax.axis_index("group")
    up = lax.rem(tile + tiles - 1, tiles)
    down = lax.rem(tile + 1, tiles)
    after = lax.rem(group + 1, groups)
    before = lax.rem(group + groups - 1, groups)

    lat_copy = [pltpu.make_async_copy(latent.at[2 * c : 2 * c + 2], lat.at[2 * c : 2 * c + 2], lat_sem.at[c]) for c in range(2)]
    wa_copy = [pltpu.make_async_copy(kernel_first.at[i], wa.at[i], w_sem.at[i]) for i in range(3)]
    wb_copy = [pltpu.make_async_copy(kernel_second.at[i], wb.at[i], w_sem.at[3 + i]) for i in range(3)]
    for copy in (lat_copy[1], lat_copy[0], *wa_copy, *wb_copy):
        copy.start()

    barrier = pltpu.get_barrier_semaphore()
    for place in ((up, group), (down, group), (tile, after), (tile, before)):
        pl.semaphore_signal(barrier, inc=1, device_id=place, device_id_type=MESH)
    pl.semaphore_wait(barrier, 4)

    live = [jnp.minimum(jnp.maximum(tile_rows[tile] - r, 0), 1).astype(F32) for r in range(rows)]

    def to_next(step, x, c):
        return pltpu.make_async_remote_copy(
            src_ref=x.at[frames + c, 1:3], dst_ref=x.at[c, 1:3],
            send_sem=send_y.at[step, c], recv_sem=recv_y.at[step, c],
            device_id=(tile, after), device_id_type=MESH,
        )

    spans = ((4, 2), (2, 2), (0, 1), (1, 1))

    def to_tile(step, x, way, c):
        at, count = spans[c]
        source, target = ((1, 3), (2, 0))[way]
        return pltpu.make_async_remote_copy(
            src_ref=x.at[at : at + count, source], dst_ref=x.at[at : at + count, target],
            send_sem=send_r.at[step, way, c], recv_sem=recv_r.at[step, way, c],
            device_id=((up, down)[way], group), device_id_type=MESH,
        )

    def rows_sent(step, x, c):
        for way in range(2):
            to_tile(step, x, way, c).start()

    def rows_here(step, x, cs):
        for c in cs:
            for way in range(2):
                to_tile(step, x, way, c).wait_recv()
        lo = min(spans[c][0] for c in cs)
        hi = max(sum(spans[c]) for c in cs)
        nothing = jnp.zeros((hi - lo, columns, channels), BF16)

        @pl.when(tile == 0)
        def _():
            x[lo:hi, 0] = nothing

        @pl.when(tile == tiles - 1)
        def _():
            x[lo:hi, 3] = nothing

    def frames_here(step, x):
        for c in range(2):
            to_next(step, x, c).wait_recv()

        @pl.when(group == 0)
        def _():
            x[0:2, 1:3] = jnp.zeros((2, 2, columns, channels), BF16)

        for c in range(2):
            rows_sent(step, x, 2 + c)

    def own(x, w, frame, wait=None):
        for tap in range(3):
            if wait is not None:
                wait[tap].wait()
            y = own_rows(x, w, frame, tap)
            for r in range(2):
                for l in range(3):
                    at = (3 * r + l) * channels
                    part = y[:, at : at + channels].reshape(2, columns, channels)
                    if tap:
                        acc[r, l] += part
                    else:
                        acc[r, l] = part

    def halo(x, w, frame):
        for r in range(2):
            y = halo_row(x, w, frame, r)
            for l in range(3):
                acc[r, l] += y[:, l * channels : (l + 1) * channels].reshape(2, columns, channels)

    def hidden(f, r):
        return shift_sum(acc[r, 0, f], acc[r, 1, f], acc[r, 2, f])

    def second(frame):
        for f in range(2):
            for r in range(2):
                xb[2 + frame + f, 1 + r] = activate(hidden(f, r), gain_second[...], live[r]).astype(BF16)

    out_copy = [pltpu.make_async_copy(outv.at[2 * c : 2 * c + 2], decoded.at[2 * c : 2 * c + 2], out_sem.at[c]) for c in range(2)]

    def finish(frame):
        for f in range(2):
            for r in range(2):
                total = lat[frame + f, r].astype(F32) + hidden(f, r)
                outv[frame + f, r] = (total * live[r]).astype(BF16)
        out_copy[frame // 2].start()

    for c in (1, 0):
        lat_copy[c].wait()
        for f in range(2 * c, 2 * c + 2):
            for r in range(2):
                xa[2 + f, 1 + r] = activate(lat[f, r].astype(F32), gain_first[...], live[r]).astype(BF16)
        if c == 1:
            for e in range(2):
                to_next(0, xa, e).start()
        rows_sent(0, xa, 1 - c)

    own(xa, wa, 2, wa_copy)
    rows_here(0, xa, (0, 1))
    halo(xa, wa, 2)
    second(2)
    for e in range(2):
        to_next(1, xb, e).start()
    rows_sent(1, xb, 0)

    frames_here(0, xa)
    own(xa, wa, 0)
    rows_here(0, xa, (2, 3))
    halo(xa, wa, 0)
    second(0)
    rows_sent(1, xb, 1)

    own(xb, wb, 2, wb_copy)
    rows_here(1, xb, (0, 1))
    halo(xb, wb, 2)
    finish(2)

    frames_here(1, xb)
    own(xb, wb, 0)
    rows_here(1, xb, (2, 3))
    halo(xb, wb, 0)
    finish(0)

    for copy in out_copy:
        copy.wait()
    for step, x in enumerate((xa, xb)):
        for e in range(2):
            to_next(step, x, e).wait_send()
        for c in range(4):
            for way in range(2):
                to_tile(step, x, way, c).wait_send()


def solution(mesh):
    tiles, groups = mesh.shape["tile"], mesh.shape["group"]

    def local(latent, tile_rows, gain_first, kernel_first, gain_second, kernel_second):
        frames, rows, columns, channels = latent.shape
        halo = (frames + 2, rows + 2, columns, channels)
        vmem = pl.BlockSpec(memory_space=pltpu.VMEM)
        away = pl.BlockSpec(memory_space=pl.ANY)
        smem = pl.BlockSpec(memory_space=pltpu.SMEM)
        dma = pltpu.SemaphoreType.DMA
        return pl.pallas_call(
            functools.partial(kernel, tiles, groups),
            out_shape=jax.ShapeDtypeStruct(latent.shape, BF16),
            in_specs=[away, smem, vmem, away, vmem, away],
            out_specs=away,
            scratch_shapes=[
                pltpu.VMEM(halo, BF16),
                pltpu.VMEM(halo, BF16),
                pltpu.VMEM(kernel_first.shape, BF16),
                pltpu.VMEM(kernel_second.shape, BF16),
                pltpu.VMEM(latent.shape, BF16),
                pltpu.VMEM((2, 3, 2, columns, channels), F32),
                pltpu.VMEM(latent.shape, BF16),
                dma((2,)),
                dma((6,)),
                dma((2,)),
                dma((2, 2)),
                dma((2, 2)),
                dma((2, 2, 4)),
                dma((2, 2, 4)),
            ],
            compiler_params=pltpu.CompilerParams(
                collective_id=0, has_side_effects=True, vmem_limit_bytes=56 * 2**20
            ),
            cost_estimate=pl.CostEstimate(
                flops=4 * 27 * frames * rows * columns * channels * channels,
                bytes_accessed=2 * (2 * latent.size + 2 * kernel_first.size),
                transcendentals=2 * latent.size,
            ),
        )(
            latent, tile_rows,
            gain_first.reshape(1, channels), kernel_first,
            gain_second.reshape(1, channels), kernel_second,
        )

    in_specs = (P("group", "tile", None, None), P(), P(), P(), P(), P())
    out_specs = P("group", "tile", None, None)
    return jax.shard_map(local, mesh=mesh, in_specs=in_specs, out_specs=out_specs, check_vma=False)
```

profile of v0, /device:TPU:0, one launch (start us, length us, event | category | flops | bytes accessed | tf_op | source)
XLA Modules:
  0.0 56.1 jit_solution(1428673680873318673)
XLA Ops:
  0.0 1.2 %reshape.6.gain_first = f32[1,384]{1,0:T(1,128)} reshape(f32[384]{0:T(512)} %param.8) | data formatting | bytes 3072 | tf_op jit(solution)/shard_map/reshape | solution.py:245
  1.2 1.3 %reshape.7.gain_second = f32[1,384]{1,0:T(1,128)} reshape(f32[384]{0:T(512)} %param.10) | data formatting | bytes 3072 | tf_op jit(solution)/shard_map/reshape | solution.py:246
  2.5 51.3 %shard_map.64 = bf16[4,2,160,384]{3,2,1,0:T(8,128)(2,1)} custom-call(bf16[4,2,160,384]{3,2,1,0:T(8,128)(2,1)} %latent.1, s32[32]{0:T(128)} %tile_rows.1, f32[1,384]{1,0:T(1,128)} %reshape.6.gain_first, bf16[3,3,3,384,384]{4,3,2,1,0:T(8,128)(2,1)} %kernel_first.1, f32[1,384]{1,0:T(1,128)} %reshape.7.gain_second, bf16[3,3,3,384,384]{4,3,2,1,0:T(8,128)(2,1)} %kernel_second.1), custom_call_target="tpu_custom_call" | custom-call | flops 20384317440 | bytes 17891328 | tf_op jit(solution)/shard_map/pallas_call | solution.py:214
  53.8 2.2 %copy.8 = bf16[4,2,160,384]{3,2,1,0:T(8,128)(2,1)} copy(bf16[4,2,160,384]{3,2,1,0:T(8,128)(2,1)} %shard_map.64) | data formatting | bytes 1966080
where the time goes:
time: 56.3 us; the launch traced here: 56.1 us
  Pallas kernels  51.3 us (91%)
  local copies, waits for them, and re-layouts  4.75 us (8%)
    pallas_call x1, Pallas kernels, local(): pl.pallas_call(functools.partial(kernel, tiles, groups), out_shape=jax.Sh...  51.3 us
    unnamed x1, local copies, waits for them, and re-layouts  2.24 us
    reshape x1, local copies, waits for them, and re-layouts, local(): gain_second.reshape(1, channels)  1.26 us
    reshape x1, local copies, waits for them, and re-layouts, local(): gain_first.reshape(1, channels)  1.24 us

commit v1 on v0

v1 whole, which is shorter than its diff:
```python
import functools

import jax
import jax.numpy as jnp
from jax import lax
from jax.experimental import pallas as pl
from jax.experimental.pallas import tpu as pltpu
from jax.sharding import PartitionSpec as P

MESH = pl.DeviceIdType.MESH
cat = jnp.concatenate
F32 = jnp.float32
BF16 = jnp.bfloat16


def activate(values, gain, live):
    scale = lax.rsqrt(jnp.mean(values * values, axis=-1, keepdims=True) + 1e-06)
    u = values * scale * gain
    return (u / (1.0 + jnp.exp(-u))) * live


def shift_sum(before, here, after):
    columns = here.shape[0]
    place = lax.broadcasted_iota(jnp.int32, here.shape, 0)
    left = jnp.where(place == 0, 0.0, pltpu.roll(before, 1, 0))
    right = jnp.where(place == columns - 1, 0.0, pltpu.roll(after, columns - 1, 0))
    return left + here + right


def own_rows(x, w, frame, tap):
    _, _, columns, channels = x.shape
    lhs = cat([x[frame + tap : frame + tap + 2, r].reshape(2 * columns, channels) for r in (1, 2)], axis=1)
    rhs = cat([cat([w[tap, r - out, l] for out in (0, 1) for l in range(3)], axis=1) for r in (1, 2)], axis=0)
    return jnp.dot(lhs, rhs, preferred_element_type=F32)


def halo_row(x, w, frame, out, taps):
    _, _, columns, channels = x.shape
    lhs = cat([x[frame + i : frame + i + 2, 3 * out].reshape(2 * columns, channels) for i in taps], axis=1)
    rhs = cat([cat([w[i, 2 * out, l] for l in range(3)], axis=1) for i in taps], axis=0)
    return jnp.dot(lhs, rhs, preferred_element_type=F32)


def kernel(
    tiles, groups,
    latent, tile_rows, gain_first, kernel_first, gain_second, kernel_second,
    decoded,
    xa, xb, wa, wb, lat, acc, outv,
    lat_sem, w_sem, out_sem, send_y, recv_y, send_r, recv_r,
):
    frames, rows, columns, channels = lat.shape
    tile = lax.axis_index("tile")
    group = lax.axis_index("group")
    above, below = tile > 0, tile < tiles - 1
    earlier, later = group > 0, group < groups - 1
    up, down = jnp.maximum(tile - 1, 0), jnp.minimum(tile + 1, tiles - 1)
    before, after = jnp.maximum(group - 1, 0), jnp.minimum(group + 1, groups - 1)

    lat_copy = [pltpu.make_async_copy(latent.at[f], lat.at[f], lat_sem.at[f]) for f in range(frames)]
    wa_copy = [pltpu.make_async_copy(kernel_first.at[i], wa.at[i], w_sem.at[i]) for i in range(3)]
    wb_copy = [pltpu.make_async_copy(kernel_second.at[i], wb.at[i], w_sem.at[3 + i]) for i in range(3)]
    out_copy = [pltpu.make_async_copy(outv.at[f], decoded.at[f], out_sem.at[f]) for f in range(frames)]
    for copy in (*lat_copy[::-1], *wa_copy[::-1], *wb_copy[::-1]):
        copy.start()

    barrier = pltpu.get_barrier_semaphore()
    around = ((above, (up, group)), (below, (down, group)), (earlier, (tile, before)), (later, (tile, after)))
    for there, place in around:

        @pl.when(there)
        def _():
            pl.semaphore_signal(barrier, inc=1, device_id=place, device_id_type=MESH)

    live = [jnp.minimum(jnp.maximum(tile_rows[tile] - r, 0), 1).astype(F32) for r in range(rows)]
    gains = [gain_first[...].reshape(1, channels), gain_second[...].reshape(1, channels)]
    xs = (xa, xb)

    def to_next(step, e):
        x = xs[step]
        return pltpu.make_async_remote_copy(
            src_ref=x.at[frames + e, 1:3], dst_ref=x.at[e, 1:3],
            send_sem=send_y.at[step, e], recv_sem=recv_y.at[step, e],
            device_id=(tile, after), device_id_type=MESH,
        )

    def to_tile(step, way, f):
        x = xs[step]
        source, target = ((1, 3), (2, 0))[way]
        return pltpu.make_async_remote_copy(
            src_ref=x.at[f, source], dst_ref=x.at[f, target],
            send_sem=send_r.at[step, way, f], recv_sem=recv_r.at[step, way, f],
            device_id=((up, down)[way], group), device_id_type=MESH,
        )

    def along(f, there):
        return there if f >= 2 else there & earlier

    def send_rows(step, f):
        for way, there in enumerate((above, below)):

            @pl.when(along(f, there))
            def _():
                to_tile(step, way, f).start()

    def wait_rows(step, fs):
        for f in fs:
            for way, there in enumerate((below, above)):

                @pl.when(along(f, there))
                def _():
                    to_tile(step, way, f).wait_recv()

    def send_frame(step, e):
        @pl.when(later)
        def _():
            to_next(step, e).start()

    def pass_frame(step, e):
        @pl.when(earlier)
        def _():
            to_next(step, e).wait_recv()

        send_rows(step, e)

    def ready(step, f):
        if f >= frames:
            send_frame(step, f - frames)
        send_rows(step, f)

    begun = set()

    def add(pair, r, l, part, fresh):
        part = part.reshape(2, columns, channels)
        if fresh:
            acc[pair, r, l] = part
        else:
            acc[pair, r, l] += part

    def own(step, frame, tap):
        x, w, pair = xs[step], (wa, wb)[step], frame // 2
        y = own_rows(x, w, frame, tap)
        for r in range(2):
            for l in range(3):
                at = (3 * r + l) * channels
                add(pair, r, l, y[:, at : at + channels], (step, pair) not in begun)
        begun.add((step, pair))

    def halo(step, frame, taps):
        x, w, pair = xs[step], (wa, wb)[step], frame // 2
        for r in range(2):
            y = halo_row(x, w, frame, r, taps)
            for l in range(3):
                add(pair, r, l, y[:, l * channels : (l + 1) * channels], False)

    def summed(f, r):
        pair, e = divmod(f, 2)
        return shift_sum(acc[pair, r, 0, e], acc[pair, r, 1, e], acc[pair, r, 2, e])

    def second(frame):
        for f in (frame + 1, frame):
            for r in range(2):
                xb[2 + f, 1 + r] = activate(summed(f, r), gains[1], live[r]).astype(BF16)
            ready(1, 2 + f)

    def finish(frame):
        for f in (frame, frame + 1):
            for r in range(2):
                total = lat[f, r].astype(F32) + summed(f, r)
                outv[f, r] = (total * live[r]).astype(BF16)
            out_copy[f].start()

    for f in reversed(range(frames)):
        lat_copy[f].wait()
        for r in range(2):
            xa[2 + f, 1 + r] = activate(lat[f, r].astype(F32), gains[0], live[r]).astype(BF16)
        if f == frames - 1:
            count = sum(there.astype(jnp.int32) for there, _ in around)
            pl.semaphore_wait(barrier, count)
        ready(0, 2 + f)

    for x in xs:

        @pl.when(jnp.logical_not(above))
        def _():
            x[:, 0] = jnp.zeros((frames + 2, columns, channels), BF16)

        @pl.when(jnp.logical_not(below))
        def _():
            x[:, 3] = jnp.zeros((frames + 2, columns, channels), BF16)

        @pl.when(jnp.logical_not(earlier))
        def _():
            x[0:2] = jnp.zeros((2, rows + 2, columns, channels), BF16)

    for tap in (2, 1, 0):
        wa_copy[tap].wait()
        own(0, 2, tap)
    own(0, 0, 2)
    wait_rows(0, (5, 4, 3, 2))
    halo(0, 2, (0, 1, 2))
    second(2)
    pass_frame(0, 1)
    wb_copy[2].wait()
    own(1, 2, 2)
    own(0, 0, 1)
    pass_frame(0, 0)
    own(0, 0, 0)
    wait_rows(0, (1,))
    halo(0, 0, (1, 2))
    wait_rows(1, (5, 4))
    halo(1, 2, (2,))
    wait_rows(0, (0,))
    halo(0, 0, (0,))
    second(0)

    wb_copy[1].wait()
    own(1, 2, 1)
    pass_frame(1, 1)
    wb_copy[0].wait()
    own(1, 2, 0)
    own(1, 0, 2)
    own(1, 0, 1)
    wait_rows(1, (3, 2))
    halo(1, 2, (0, 1))
    finish(2)
    pass_frame(1, 0)
    own(1, 0, 0)
    wait_rows(1, (1,))
    halo(1, 0, (1, 2))
    wait_rows(1, (0,))
    halo(1, 0, (0,))
    finish(0)

    for copy in out_copy:
        copy.wait()
    for step in range(2):
        for e in range(2):

            @pl.when(later)
            def _():
                to_next(step, e).wait_send()

        for f in range(frames + 2):
            for way, there in enumerate((above, below)):

                @pl.when(along(f, there))
                def _():
                    to_tile(step, way, f).wait_send()


def solution(mesh):
    tiles, groups = mesh.shape["tile"], mesh.shape["group"]

    def local(latent, tile_rows, gain_first, kernel_first, gain_second, kernel_second):
        frames, rows, columns, channels = latent.shape
        halo = (frames + 2, rows + 2, columns, channels)
        vmem = pl.BlockSpec(memory_space=pltpu.VMEM)
        away = pl.BlockSpec(memory_space=pl.ANY)
        smem = pl.BlockSpec(memory_space=pltpu.SMEM)
        dma = pltpu.SemaphoreType.DMA
        return pl.pallas_call(
            functools.partial(kernel, tiles, groups),
            out_shape=jax.ShapeDtypeStruct(latent.shape, BF16),
            in_specs=[away, smem, vmem, away, vmem, away],
            out_specs=away,
            scratch_shapes=[
                pltpu.VMEM(halo, BF16),
                pltpu.VMEM(halo, BF16),
                pltpu.VMEM(kernel_first.shape, BF16),
                pltpu.VMEM(kernel_second.shape, BF16),
                pltpu.VMEM(latent.shape, BF16),
                pltpu.VMEM((2, 2, 3, 2, columns, channels), F32),
                pltpu.VMEM(latent.shape, BF16),
                dma((frames,)),
                dma((6,)),
                dma((frames,)),
                dma((2, 2)),
                dma((2, 2)),
                dma((2, 2, frames + 2)),
                dma((2, 2, frames + 2)),
            ],
            compiler_params=pltpu.CompilerParams(
                collective_id=0, has_side_effects=True, vmem_limit_bytes=56 * 2**20
            ),
            cost_estimate=pl.CostEstimate(
                flops=4 * 27 * frames * rows * columns * channels * channels,
                bytes_accessed=2 * (2 * latent.size + 2 * kernel_first.size),
                transcendentals=2 * latent.size,
            ),
        )(
            latent, tile_rows,
            gain_first, kernel_first,
            gain_second, kernel_second,
        )

    in_specs = (P("group", "tile", None, None), P(), P(), P(), P(), P())
    out_specs = P("group", "tile", None, None)
    return jax.shard_map(local, mesh=mesh, in_specs=in_specs, out_specs=out_specs, check_vma=False)
```

time: 56.3 us -> 42.9 us (0.76)
  the two profiles are of different devices: /device:TPU:0 before, /device:TPU:95 now
where the time goes in v1:
time: 42.9 us; the launch traced here: 42.7 us
  Pallas kernels  40.5 us (94%)
  local copies, waits for them, and re-layouts  2.24 us (5%)
    pallas_call x1, Pallas kernels, local(): pl.pallas_call(functools.partial(kernel, tiles, groups), out_shape=jax.Sh...  40.5 us
    unnamed x1, local copies, waits for them, and re-layouts  2.24 us

profile of v1, /device:TPU:95, one launch (start us, length us, event | category | flops | bytes accessed | tf_op | source)
XLA Modules:
  0.0 42.7 jit_solution(15003102697090347298)
XLA Ops:
  0.0 40.5 %shard_map.64 = bf16[4,2,160,384]{3,2,1,0:T(8,128)(2,1)} custom-call(bf16[4,2,160,384]{3,2,1,0:T(8,128)(2,1)} %latent.1, s32[32]{0:T(128)} %tile_rows.1, f32[384]{0:T(512)} %gain_first.1, bf16[3,3,3,384,384]{4,3,2,1,0:T(8,128)(2,1)} %kernel_first.1, f32[384]{0:T(512)} %gain_second.1, bf16[3,3,3,384,384]{4,3,2,1,0:T(8,128)(2,1)} %kernel_second.1), custom_call_target="tpu_custom_call" | custom-call | flops 20384317440 | bytes 17891328 | tf_op jit(solution)/shard_map/pallas_call | solution.py:261
  40.5 2.2 %copy.8 = bf16[4,2,160,384]{3,2,1,0:T(8,128)(2,1)} copy(bf16[4,2,160,384]{3,2,1,0:T(8,128)(2,1)} %shard_map.64) | data formatting | bytes 1966080

commit v2 on v1

--- a/solution.py
+++ b/solution.py
@@ -27,16 +27,17 @@
     return left + here + right
 
 
-def own_rows(x, w, frame, tap):
+def own_rows(x, w, frame, count, tap):
     _, _, columns, channels = x.shape
-    lhs = cat([x[frame + tap : frame + tap + 2, r].reshape(2 * columns, channels) for r in (1, 2)], axis=1)
+    at = frame + tap
+    lhs = cat([x[at : at + count, r].reshape(count * columns, channels) for r in (1, 2)], axis=1)
     rhs = cat([cat([w[tap, r - out, l] for out in (0, 1) for l in range(3)], axis=1) for r in (1, 2)], axis=0)
     return jnp.dot(lhs, rhs, preferred_element_type=F32)
 
 
-def halo_row(x, w, frame, out, taps):
+def halo_row(x, w, frame, count, out, taps):
     _, _, columns, channels = x.shape
-    lhs = cat([x[frame + i : frame + i + 2, 3 * out].reshape(2 * columns, channels) for i in taps], axis=1)
+    lhs = cat([x[frame + i : frame + i + count, 3 * out].reshape(count * columns, channels) for i in taps], axis=1)
     rhs = cat([cat([w[i, 2 * out, l] for l in range(3)], axis=1) for i in taps], axis=0)
     return jnp.dot(lhs, rhs, preferred_element_type=F32)
 
@@ -60,7 +61,7 @@
     wa_copy = [pltpu.make_async_copy(kernel_first.at[i], wa.at[i], w_sem.at[i]) for i in range(3)]
     wb_copy = [pltpu.make_async_copy(kernel_second.at[i], wb.at[i], w_sem.at[3 + i]) for i in range(3)]
     out_copy = [pltpu.make_async_copy(outv.at[f], decoded.at[f], out_sem.at[f]) for f in range(frames)]
-    for copy in (*lat_copy[::-1], *wa_copy[::-1], *wb_copy[::-1]):
+    for copy in (*lat_copy[::-1], wa_copy[2]):
         copy.start()
 
     barrier = pltpu.get_barrier_semaphore()
@@ -127,47 +128,41 @@
             send_frame(step, f - frames)
         send_rows(step, f)
 
-    begun = set()
-
-    def add(pair, r, l, part, fresh):
-        part = part.reshape(2, columns, channels)
+    def add(frame, count, r, l, part, fresh):
+        pair, e = divmod(frame, 2)
+        part = part.reshape(count, columns, channels)
         if fresh:
-            acc[pair, r, l] = part
+            acc[pair, r, l, e : e + count] = part
         else:
-            acc[pair, r, l] += part
-
-    def own(step, frame, tap):
-        x, w, pair = xs[step], (wa, wb)[step], frame // 2
-        y = own_rows(x, w, frame, tap)
+            acc[pair, r, l, e : e + count] += part
+
+    def own(step, frame, count, tap):
+        y = own_rows(xs[step], (wa, wb)[step], frame, count, tap)
         for r in range(2):
             for l in range(3):
                 at = (3 * r + l) * channels
-                add(pair, r, l, y[:, at : at + channels], (step, pair) not in begun)
-        begun.add((step, pair))
-
-    def halo(step, frame, taps):
-        x, w, pair = xs[step], (wa, wb)[step], frame // 2
-        for r in range(2):
-            y = halo_row(x, w, frame, r, taps)
+                add(frame, count, r, l, y[:, at : at + channels], tap == 2)
+
+    def halo(step, frame, count, taps):
+        for r in range(2):
+            y = halo_row(xs[step], (wa, wb)[step], frame, count, r, taps)
             for l in range(3):
-                add(pair, r, l, y[:, l * channels : (l + 1) * channels], False)
+                add(frame, count, r, l, y[:, l * channels : (l + 1) * channels], False)
 
     def summed(f, r):
         pair, e = divmod(f, 2)
         return shift_sum(acc[pair, r, 0, e], acc[pair, r, 1, e], acc[pair, r, 2, e])
 
-    def second(frame):
-        for f in (frame + 1, frame):
-            for r in range(2):
-                xb[2 + f, 1 + r] = activate(summed(f, r), gains[1], live[r]).astype(BF16)
-            ready(1, 2 + f)
-
-    def finish(frame):
-        for f in (frame, frame + 1):
-            for r in range(2):
-                total = lat[f, r].astype(F32) + summed(f, r)
-                outv[f, r] = (total * live[r]).astype(BF16)
-            out_copy[f].start()
+    def second(f):
+        for r in range(2):
+            xb[2 + f, 1 + r] = activate(summed(f, r), gains[1], live[r]).astype(BF16)
+        ready(1, 2 + f)
+
+    def finish(f):
+        for r in range(2):
+            total = lat[f, r].astype(F32) + summed(f, r)
+            outv[f, r] = (total * live[r]).astype(BF16)
+        out_copy[f].start()
 
     for f in reversed(range(frames)):
         lat_copy[f].wait()
@@ -177,6 +172,8 @@
             count = sum(there.astype(jnp.int32) for there, _ in around)
             pl.semaphore_wait(barrier, count)
         ready(0, 2 + f)
+        if f >= 2:
+            wa_copy[f - 2].start()
 
     for x in xs:
 
@@ -194,41 +191,52 @@
 
     for tap in (2, 1, 0):
         wa_copy[tap].wait()
-        own(0, 2, tap)
-    own(0, 0, 2)
-    wait_rows(0, (5, 4, 3, 2))
-    halo(0, 2, (0, 1, 2))
+        own(0, 2, 2, tap)
+        wb_copy[tap].start()
+    own(0, 0, 2, 2)
+    wait_rows(0, (5, 4))
+    halo(0, 2, 2, (2,))
+    pass_frame(0, 1)
+    own(0, 0, 2, 1)
+    wait_rows(0, (3, 2))
+    halo(0, 2, 2, (0, 1))
+    second(3)
     second(2)
-    pass_frame(0, 1)
     wb_copy[2].wait()
-    own(1, 2, 2)
-    own(0, 0, 1)
+    own(1, 2, 2, 2)
+    own(0, 1, 1, 0)
     pass_frame(0, 0)
-    own(0, 0, 0)
     wait_rows(0, (1,))
-    halo(0, 0, (1, 2))
+    halo(0, 0, 2, (1, 2))
+    halo(0, 1, 1, (0,))
+    second(1)
+    wb_copy[1].wait()
+    own(1, 2, 2, 1)
     wait_rows(1, (5, 4))
-    halo(1, 2, (2,))
+    halo(1, 2, 2, (2,))
+    own(0, 0, 1, 0)
     wait_rows(0, (0,))
-    halo(0, 0, (0,))
+    halo(0, 0, 1, (0,))
     second(0)
 
-    wb_copy[1].wait()
-    own(1, 2, 1)
+    own(1, 0, 2, 2)
     pass_frame(1, 1)
     wb_copy[0].wait()
-    own(1, 2, 0)
-    own(1, 0, 2)
-    own(1, 0, 1)
+    own(1, 2, 2, 0)
+    own(1, 0, 2, 1)
     wait_rows(1, (3, 2))
-    halo(1, 2, (0, 1))
+    halo(1, 2, 2, (0, 1))
+    finish(3)
     finish(2)
     pass_frame(1, 0)
-    own(1, 0, 0)
     wait_rows(1, (1,))
-    halo(1, 0, (1, 2))
+    halo(1, 0, 2, (1, 2))
+    own(1, 1, 1, 0)
+    halo(1, 1, 1, (0,))
+    finish(1)
+    own(1, 0, 1, 0)
     wait_rows(1, (0,))
-    halo(1, 0, (0,))
+    halo(1, 0, 1, (0,))
     finish(0)
 
     for copy in out_copy:

time: 42.9 us -> 37.8 us (0.88); the launches traced: 42.7 us -> 37 us
  Pallas kernels: 40.5 us -> 34.8 us
    pallas_call x1, Pallas kernels: 40.5 us -> 34.8 us  [local(): pl.pallas_call(functools.partial(kernel, tiles, groups), out_shape=jax.Sh...]
where the time goes in v2:
time: 37.8 us; the launch traced here: 37 us
  Pallas kernels  34.8 us (92%)
  local copies, waits for them, and re-layouts  2.24 us (6%)
    pallas_call x1, Pallas kernels, local(): pl.pallas_call(functools.partial(kernel, tiles, groups), out_shape=jax.Sh...  34.8 us
    unnamed x1, local copies, waits for them, and re-layouts  2.24 us

profile of v2, /device:TPU:95, one launch (start us, length us, event | category | flops | bytes accessed | tf_op | source)
XLA Modules:
  0.0 37.0 jit_solution(2323004478649502395)
XLA Ops:
  0.0 34.8 %shard_map.64 = bf16[4,2,160,384]{3,2,1,0:T(8,128)(2,1)} custom-call(bf16[4,2,160,384]{3,2,1,0:T(8,128)(2,1)} %latent.1, s32[32]{0:T(128)} %tile_rows.1, f32[384]{0:T(512)} %gain_first.1, bf16[3,3,3,384,384]{4,3,2,1,0:T(8,128)(2,1)} %kernel_first.1, f32[384]{0:T(512)} %gain_second.1, bf16[3,3,3,384,384]{4,3,2,1,0:T(8,128)(2,1)} %kernel_second.1), custom_call_target="tpu_custom_call" | custom-call | flops 20384317440 | bytes 17891328 | tf_op jit(solution)/shard_map/pallas_call | solution.py:269
  34.8 2.2 %copy.8 = bf16[4,2,160,384]{3,2,1,0:T(8,128)(2,1)} copy(bf16[4,2,160,384]{3,2,1,0:T(8,128)(2,1)} %shard_map.64) | data formatting | bytes 1966080

commit v3 on v2

--- a/solution.py
+++ b/solution.py
@@ -46,8 +46,8 @@
     tiles, groups,
     latent, tile_rows, gain_first, kernel_first, gain_second, kernel_second,
     decoded,
-    xa, xb, wa, wb, lat, acc, outv,
-    lat_sem, w_sem, out_sem, send_y, recv_y, send_r, recv_r,
+    xa, xb, wa, wb, lat, acc,
+    lat_sem, w_sem, send_y, recv_y, send_r, recv_r,
 ):
     frames, rows, columns, channels = lat.shape
     tile = lax.axis_index("tile")
@@ -60,7 +60,6 @@
     lat_copy = [pltpu.make_async_copy(latent.at[f], lat.at[f], lat_sem.at[f]) for f in range(frames)]
     wa_copy = [pltpu.make_async_copy(kernel_first.at[i], wa.at[i], w_sem.at[i]) for i in range(3)]
     wb_copy = [pltpu.make_async_copy(kernel_second.at[i], wb.at[i], w_sem.at[3 + i]) for i in range(3)]
-    out_copy = [pltpu.make_async_copy(outv.at[f], decoded.at[f], out_sem.at[f]) for f in range(frames)]
     for copy in (*lat_copy[::-1], wa_copy[2]):
         copy.start()
 
@@ -161,8 +160,7 @@
     def finish(f):
         for r in range(2):
             total = lat[f, r].astype(F32) + summed(f, r)
-            outv[f, r] = (total * live[r]).astype(BF16)
-        out_copy[f].start()
+            decoded[f, r] = (total * live[r]).astype(BF16)
 
     for f in reversed(range(frames)):
         lat_copy[f].wait()
@@ -224,11 +222,11 @@
     wb_copy[0].wait()
     own(1, 2, 2, 0)
     own(1, 0, 2, 1)
+    pass_frame(1, 0)
     wait_rows(1, (3, 2))
     halo(1, 2, 2, (0, 1))
     finish(3)
     finish(2)
-    pass_frame(1, 0)
     wait_rows(1, (1,))
     halo(1, 0, 2, (1, 2))
     own(1, 1, 1, 0)
@@ -239,8 +237,6 @@
     halo(1, 0, 1, (0,))
     finish(0)
 
-    for copy in out_copy:
-        copy.wait()
     for step in range(2):
         for e in range(2):
 
@@ -268,9 +264,9 @@
         dma = pltpu.SemaphoreType.DMA
         return pl.pallas_call(
             functools.partial(kernel, tiles, groups),
-            out_shape=jax.ShapeDtypeStruct(latent.shape, BF16),
+            out_shape=pltpu.VMEM(latent.shape, BF16),
             in_specs=[away, smem, vmem, away, vmem, away],
-            out_specs=away,
+            out_specs=pl.BlockSpec(memory_space=pltpu.VMEM),
             scratch_shapes=[
                 pltpu.VMEM(halo, BF16),
                 pltpu.VMEM(halo, BF16),
@@ -278,10 +274,8 @@
                 pltpu.VMEM(kernel_second.shape, BF16),
                 pltpu.VMEM(latent.shape, BF16),
                 pltpu.VMEM((2, 2, 3, 2, columns, channels), F32),
-                pltpu.VMEM(latent.shape, BF16),
                 dma((frames,)),
                 dma((6,)),
-                dma((frames,)),
                 dma((2, 2)),
                 dma((2, 2)),
                 dma((2, 2, frames + 2)),

time: 37.8 us -> 34.4 us (0.910); the launches traced: 37 us -> 34.2 us
  Pallas kernels: 34.8 us -> 33.2 us
  local copies, waits for them, and re-layouts: 2.24 us -> 0.95 us
    pallas_call x1, Pallas kernels: 34.8 us -> 33.2 us  [local(): pl.pallas_call(functools.partial(kernel, tiles, groups), out_shape=pltpu....]
    unnamed x1, local copies, waits for them, and re-layouts: 2.24 us -> 0.95 us
where the time goes in v3:
time: 34.4 us; the launch traced here: 34.2 us
  Pallas kernels  33.2 us (97%)
  local copies, waits for them, and re-layouts  0.95 us (3%)
    pallas_call x1, Pallas kernels, local(): pl.pallas_call(functools.partial(kernel, tiles, groups), out_shape=pltpu....  33.2 us
    unnamed x1, local copies, waits for them, and re-layouts  0.95 us

profile of v3, /device:TPU:95, one launch (start us, length us, event | category | flops | bytes accessed | tf_op | source)
XLA Modules:
  0.0 34.2 jit_solution(450800040025235788)
XLA Ops:
  0.0 33.2 %shard_map.64 = bf16[4,2,160,384]{3,2,1,0:T(8,128)(2,1)S(1)} custom-call(bf16[4,2,160,384]{3,2,1,0:T(8,128)(2,1)} %latent.1, s32[32]{0:T(128)} %tile_rows.1, f32[384]{0:T(512)} %gain_first.1, bf16[3,3,3,384,384]{4,3,2,1,0:T(8,128)(2,1)} %kernel_first.1, f32[384]{0:T(512)} %gain_second.1, bf16[3,3,3,384,384]{4,3,2,1,0:T(8,128)(2,1)} %kernel_second.1), custom_call_target="tpu_custom_call" | custom-call | flops 20384317440 | bytes 17891328 | tf_op jit(solution)/shard_map/pallas_call | solution.py:265
  33.2 0.9 %copy.8 = bf16[4,2,160,384]{3,2,1,0:T(8,128)(2,1)} copy(bf16[4,2,160,384]{3,2,1,0:T(8,128)(2,1)S(1)} %shard_map.64) | data formatting | bytes 1966080

commit v4 on v3

--- a/solution.py
+++ b/solution.py
@@ -15,8 +15,8 @@
 
 def activate(values, gain, live):
     scale = lax.rsqrt(jnp.mean(values * values, axis=-1, keepdims=True) + 1e-06)
-    u = values * scale * gain
-    return (u / (1.0 + jnp.exp(-u))) * live
+    h = values * scale * (0.5 * gain)
+    return (h + h * jnp.tanh(h)) * live
 
 
 def shift_sum(before, here, after):
@@ -60,9 +60,6 @@
     lat_copy = [pltpu.make_async_copy(latent.at[f], lat.at[f], lat_sem.at[f]) for f in range(frames)]
     wa_copy = [pltpu.make_async_copy(kernel_first.at[i], wa.at[i], w_sem.at[i]) for i in range(3)]
     wb_copy = [pltpu.make_async_copy(kernel_second.at[i], wb.at[i], w_sem.at[3 + i]) for i in range(3)]
-    for copy in (*lat_copy[::-1], wa_copy[2]):
-        copy.start()
-
     barrier = pltpu.get_barrier_semaphore()
     around = ((above, (up, group)), (below, (down, group)), (earlier, (tile, before)), (later, (tile, after)))
     for there, place in around:
@@ -71,24 +68,27 @@
         def _():
             pl.semaphore_signal(barrier, inc=1, device_id=place, device_id_type=MESH)
 
+    for copy in (*lat_copy[::-1], wa_copy[2]):
+        copy.start()
+
     live = [jnp.minimum(jnp.maximum(tile_rows[tile] - r, 0), 1).astype(F32) for r in range(rows)]
     gains = [gain_first[...].reshape(1, channels), gain_second[...].reshape(1, channels)]
     xs = (xa, xb)
 
-    def to_next(step, e):
+    def to_next(step, e, count=1):
         x = xs[step]
         return pltpu.make_async_remote_copy(
-            src_ref=x.at[frames + e, 1:3], dst_ref=x.at[e, 1:3],
-            send_sem=send_y.at[step, e], recv_sem=recv_y.at[step, e],
+            src_ref=x.at[frames + e : frames + e + count, 1:3], dst_ref=x.at[e : e + count, 1:3],
+            send_sem=send_y.at[step], recv_sem=recv_y.at[step, e],
             device_id=(tile, after), device_id_type=MESH,
         )
 
-    def to_tile(step, way, f):
+    def to_tile(step, way, f, count=1):
         x = xs[step]
         source, target = ((1, 3), (2, 0))[way]
         return pltpu.make_async_remote_copy(
-            src_ref=x.at[f, source], dst_ref=x.at[f, target],
-            send_sem=send_r.at[step, way, f], recv_sem=recv_r.at[step, way, f],
+            src_ref=x.at[f : f + count, source], dst_ref=x.at[f : f + count, target],
+            send_sem=send_r.at[step, way, min(f // 2, 1)], recv_sem=recv_r.at[step, way, f if f < 2 else 1 + f // 2],
             device_id=((up, down)[way], group), device_id_type=MESH,
         )
 
@@ -103,12 +103,11 @@
                 to_tile(step, way, f).start()
 
     def wait_rows(step, fs):
-        for f in fs:
-            for way, there in enumerate((below, above)):
-
-                @pl.when(along(f, there))
-                def _():
-                    to_tile(step, way, f).wait_recv()
+        for way, there in enumerate((below, above)):
+
+            @pl.when(along(fs[-1], there))
+            def _():
+                to_tile(step, way, fs[-1], len(fs)).wait_recv()
 
     def send_frame(step, e):
         @pl.when(later)
@@ -238,18 +237,20 @@
     finish(0)
 
     for step in range(2):
-        for e in range(2):
-
-            @pl.when(later)
+
+        @pl.when(later)
+        def _():
+            to_next(step, 0, 2).wait_send()
+
+        for way, there in enumerate((above, below)):
+
+            @pl.when(there)
             def _():
-                to_next(step, e).wait_send()
-
-        for f in range(frames + 2):
-            for way, there in enumerate((above, below)):
-
-                @pl.when(along(f, there))
-                def _():
-                    to_tile(step, way, f).wait_send()
+                to_tile(step, way, 2, frames).wait_send()
+
+            @pl.when(there & earlier)
+            def _():
+                to_tile(step, way, 0, 2).wait_send()
 
 
 def solution(mesh):
@@ -276,10 +277,10 @@
                 pltpu.VMEM((2, 2, 3, 2, columns, channels), F32),
                 dma((frames,)),
                 dma((6,)),
+                dma((2,)),
                 dma((2, 2)),
-                dma((2, 2)),
-                dma((2, 2, frames + 2)),
-                dma((2, 2, frames + 2)),
+                dma((2, 2, 2)),
+                dma((2, 2, 4)),
             ],
             compiler_params=pltpu.CompilerParams(
                 collective_id=0, has_side_effects=True, vmem_limit_bytes=56 * 2**20

time: 34.4 us -> 33.9 us (0.985)
  Pallas kernels: 33.2 us -> 32.8 us
    pallas_call x1, Pallas kernels: 33.2 us -> 32.8 us  [local(): pl.pallas_call(functools.partial(kernel, tiles, groups), out_shape=pltpu....]
where the time goes in v4:
time: 33.9 us; the launch traced here: 33.8 us
  Pallas kernels  32.8 us (97%)
  local copies, waits for them, and re-layouts  0.95 us (3%)
    pallas_call x1, Pallas kernels, local(): pl.pallas_call(functools.partial(kernel, tiles, groups), out_shape=pltpu....  32.8 us
    unnamed x1, local copies, waits for them, and re-layouts  0.95 us

profile of v4, /device:TPU:95, one launch (start us, length us, event | category | flops | bytes accessed | tf_op | source)
XLA Modules:
  0.0 33.8 jit_solution(5655108687994112684)
XLA Ops:
  0.0 32.8 %shard_map.64 = bf16[4,2,160,384]{3,2,1,0:T(8,128)(2,1)S(1)} custom-call(bf16[4,2,160,384]{3,2,1,0:T(8,128)(2,1)} %latent.1, s32[32]{0:T(128)} %tile_rows.1, f32[384]{0:T(512)} %gain_first.1, bf16[3,3,3,384,384]{4,3,2,1,0:T(8,128)(2,1)} %kernel_first.1, f32[384]{0:T(512)} %gain_second.1, bf16[3,3,3,384,384]{4,3,2,1,0:T(8,128)(2,1)} %kernel_second.1), custom_call_target="tpu_custom_call" | custom-call | flops 20384317440 | bytes 17891328 | tf_op jit(solution)/shard_map/pallas_call | solution.py:266
  32.8 0.9 %copy.8 = bf16[4,2,160,384]{3,2,1,0:T(8,128)(2,1)} copy(bf16[4,2,160,384]{3,2,1,0:T(8,128)(2,1)S(1)} %shard_map.64) | data formatting | bytes 1966080

commit v5 on v4

--- a/solution.py
+++ b/solution.py
@@ -224,10 +224,10 @@
     pass_frame(1, 0)
     wait_rows(1, (3, 2))
     halo(1, 2, 2, (0, 1))
+    wait_rows(1, (1,))
     finish(3)
+    halo(1, 0, 2, (1, 2))
     finish(2)
-    wait_rows(1, (1,))
-    halo(1, 0, 2, (1, 2))
     own(1, 1, 1, 0)
     halo(1, 1, 1, (0,))
     finish(1)

time: 33.9 us -> 34.3 us (1.012)
  Pallas kernels: 32.8 us -> 33.2 us
    pallas_call x1, Pallas kernels: 32.8 us -> 33.2 us  [local(): pl.pallas_call(functools.partial(kernel, tiles, groups), out_shape=pltpu....]
where the time goes in v5:
time: 34.3 us; the launch traced here: 34.2 us
  Pallas kernels  33.2 us (97%)
  local copies, waits for them, and re-layouts  0.95 us (3%)
    pallas_call x1, Pallas kernels, local(): pl.pallas_call(functools.partial(kernel, tiles, groups), out_shape=pltpu....  33.2 us
    unnamed x1, local copies, waits for them, and re-layouts  0.95 us

profile of v5, /device:TPU:95, one launch (start us, length us, event | category | flops | bytes accessed | tf_op | source)
XLA Modules:
  0.0 34.2 jit_solution(10997737994219319865)
XLA Ops:
  0.0 33.2 %shard_map.64 = bf16[4,2,160,384]{3,2,1,0:T(8,128)(2,1)S(1)} custom-call(bf16[4,2,160,384]{3,2,1,0:T(8,128)(2,1)} %latent.1, s32[32]{0:T(128)} %tile_rows.1, f32[384]{0:T(512)} %gain_first.1, bf16[3,3,3,384,384]{4,3,2,1,0:T(8,128)(2,1)} %kernel_first.1, f32[384]{0:T(512)} %gain_second.1, bf16[3,3,3,384,384]{4,3,2,1,0:T(8,128)(2,1)} %kernel_second.1), custom_call_target="tpu_custom_call" | custom-call | flops 20384317440 | bytes 17891328 | tf_op jit(solution)/shard_map/pallas_call | solution.py:266
  33.2 0.9 %copy.8 = bf16[4,2,160,384]{3,2,1,0:T(8,128)(2,1)} copy(bf16[4,2,160,384]{3,2,1,0:T(8,128)(2,1)S(1)} %shard_map.64) | data formatting | bytes 1966080
